TPU v7x, 32 devices: a whole 2x2x4 slice. The times are simulated.
32 devices in a mesh: expert: 16 (over z, y, x), tensor: 2 (over core).
Axes of the slice: x: 2, y: 2, z: 4, core: 2. Of those that a mesh axis runs over, the one named last changes fastest.
Arguments:
- grad_out: bfloat16 [8192, 3072], P('expert', 'tensor'), may hold values from -6 to 6
- hidden_in: bfloat16 [8192, 4096], P('expert', 'tensor')
- gate_prob: float32 [8192], P('expert'), may hold values from 0.1 to 1
- expert_ids: int32 [8192, 1], P('expert'), may hold values from 0 to 15; in each aligned block of 512 rows (0 to 511, 512 to 1023, ...) at most 64 rows name the same one
- w_down: bfloat16 [16, 4096, 3072], P('expert', 'tensor'), may hold values from -0.09375 to 0.09375
Outputs:
- grad_hidden: bfloat16 [8192, 4096], P('expert', 'tensor')
- grad_gate: float32 [8192], P('expert')
Inputs may be any that keep to these rules, and one draw needn't show every extreme that they name: `expert_ids`: in each aligned block of 512 tokens no expert is named more than 64 times, a bound that some block reaches.
All inputs are finite; a program needn't handle non-finite values.
Results may differ from a plain program's by a relative error of at most 0.0049.
Values may be sent and summed in bfloat16 or wider, within the bound.
A program may use at most 64 MiB of HBM per device.

v0:
```python
import jax
import jax.numpy as jnp
from jax import lax
from jax.sharding import PartitionSpec as P


def token_slots(expert_ids, experts, capacity):
    chosen = expert_ids[:, 0]
    onehot = (chosen[:, None] == jnp.arange(experts, dtype=jnp.int32)[None, :]).astype(jnp.int32)
    earlier = jnp.sum((jnp.cumsum(onehot, axis=0) - 1) * onehot, axis=1)
    return chosen * capacity + earlier


def body(grad_out, hidden_in, gate_prob, expert_ids, w_down):
    tokens = grad_out.shape[0]
    groups = lax.axis_size("expert")
    local = w_down.shape[0]
    experts = local * groups
    capacity = 2 * tokens // experts
    target = token_slots(expert_ids, experts, capacity)
    source = (
        jnp.full((experts * capacity,), tokens, jnp.int32)
        .at[target]
        .set(jnp.arange(tokens, dtype=jnp.int32))
    )
    outgoing = lax.all_gather(grad_out, "tensor", axis=1, tiled=True)
    padded = jnp.concatenate([outgoing, jnp.zeros((1, outgoing.shape[1]), outgoing.dtype)], axis=0)
    send = padded[source].reshape(experts, capacity, outgoing.shape[1])
    received = lax.all_to_all(send, "expert", split_axis=0, concat_axis=0, tiled=True)
    slots = received.shape[1]
    shaped = received.reshape(groups, local, slots, received.shape[2])
    product = jnp.einsum("sxcd,xfd->sxcf", shaped, w_down, preferred_element_type=jnp.float32)
    returned_rows = lax.all_to_all(
        product.astype(jnp.bfloat16).reshape(experts, slots, w_down.shape[1]),
        "expert",
        split_axis=0,
        concat_axis=0,
        tiled=True,
    )
    flat = returned_rows.reshape(experts * capacity, returned_rows.shape[2])
    returned = flat[target].astype(jnp.float32)
    grad_hidden = (gate_prob[:, None] * returned).astype(jnp.bfloat16)
    partial_sum = jnp.sum(hidden_in.astype(jnp.float32) * returned, axis=1)
    grad_gate = lax.psum(partial_sum, "tensor")
    return (grad_hidden, grad_gate)


def solution(mesh):
    return jax.shard_map(
        body,
        mesh=mesh,
        in_specs=(
            P("expert", "tensor"),
            P("expert", "tensor"),
            P("expert"),
            P("expert", None),
            P("expert", "tensor", None),
        ),
        out_specs=(P("expert", "tensor"), P("expert")),
        check_vma=False,
    )
```

profile of v0, /device:TPU:9, one launch (start us, length us, event | category | flops | bytes accessed | tf_op | source)
XLA Modules:
  0.0 309.8 jit_solution(16475151329034387591)
XLA Ops:
  7.2 0.0 all-gather.2.cloned.1.call-start
  7.2 0.7 all-gather.2.cloned.1.call-update
  7.9 0.7 fusion.9
  8.6 1.1 reduce-window.6
  9.7 0.2 slice_reduce_fusion
  10.0 0.8 fusion.8
  10.8 0.7 compare_select_fusion
  11.5 2.4 scatter_custom_fusion
  13.9 9.7 %all-gather.2.cloned.1.call-done = bf16[512,3072]{1,0:T(8,128)(2,1)} async-done(((bf16[512,1536]{1,0:T(8,128)(2,1)}), bf16[512,3072]{1,0:T(8,128)(2,1)}) %all-gather.2.cloned.1.call-update) | async-done | bytes 3145744 | tf_op jit(solution)/shard_map/all_gather | solution.py:26
  23.6 2.1 concatenate.3
  25.7 6.8 %gather_fusion = bf16[1024,3072]{1,0:T(8,128)(2,1)} fusion(bf16[513,3072]{1,0:T(8,128)(2,1)S(1)} %concatenate.3, s32[1024]{0:T(1024)S(1)} %fusion.10), kind=kCustom, calls=%fused_computation | custom fusion | bytes 12587008 | tf_op jit(solution)/shard_map/gather | solution.py:28
  32.5 143.7 %all_to_all.10 = bf16[16,64,3072]{2,1,0:T(8,128)(2,1)S(1)} all-to-all(bf16[16,64,3072]{2,1,0:T(8,128)(2,1)} %bitcast.28), channel_id=1, replica_groups=mesh['expert'=16,'tensor'=2] {'expert'}, dimensions={0} | all-to-all | bytes 12582912 | tf_op jit(solution)/shard_map/all_to_all | solution.py:29
  176.2 17.5 %fusion.4 = bf16[16,64,2048]{2,1,0:T(8,128)(2,1)} fusion(bf16[16,64,3072]{2,1,0:T(8,128)(2,1)S(1)} %all_to_all.10, bf16[1,2048,3072]{2,1,0:T(8,128)(2,1)} %param.9), kind=kOutput, calls=%fused_computation.9 | convolution fusion | flops 12886999040 | bytes 23068672 | tf_op jit(solution)/shard_map/sxcd,xfd->sxcf/dot_general | solution.py:32
  193.8 4.6 %all-to-all-start.1 = ((bf16[16,64,2048]{2,1,0:T(8,128)(2,1)}), bf16[16,64,2048]{2,1,0:T(8,128)(2,1)}, u32[]{:S(2)}, u32[]{:S(2)}) async-start(bf16[16,64,2048]{2,1,0:T(8,128)(2,1)} %fusion.4), calls=%async_computation.1 | async-start | bytes 8388608 | tf_op jit(solution)/shard_map/all_to_all | solution.py:33
  198.3 88.2 %all-to-all-done.1 = bf16[16,64,2048]{2,1,0:T(8,128)(2,1)} async-done(((bf16[16,64,2048]{2,1,0:T(8,128)(2,1)}), bf16[16,64,2048]{2,1,0:T(8,128)(2,1)}, u32[]{:S(2)}, u32[]{:S(2)}) %all-to-all-start.1) | async-done | bytes 4194336 | tf_op jit(solution)/shard_map/all_to_all | solution.py:33
  286.6 0.0 copy-start
  286.6 7.1 %gather_fusion.1 = bf16[512,2048]{1,0:T(8,128)(2,1)S(1)} fusion(bf16[1024,2048]{1,0:T(8,128)(2,1)} %bitcast.8, s32[1024]{0:T(1024)S(1)} %pad_clamp_fusion), kind=kCustom, calls=%fused_computation.1 | custom fusion | bytes 4196352 | tf_op jit(solution)/shard_map/gather | solution.py:41
  293.7 0.0 copy-done
  293.7 3.7 %fusion.3 = (f32[512]{0:T(512)S(1)}, bf16[512,2048]{1,0:T(8,128)(2,1)}) fusion(bf16[512,2048]{1,0:T(8,128)(2,1)S(1)} %gather_fusion.1, bf16[512,2048]{1,0:T(8,128)(2,1)} %param.6, f32[512]{0:T(512)S(1)} %copy-done), kind=kLoop, calls=%fused_computation.8 | loop fusion | flops 6290944 | bytes 6295552 | tf_op jit(solution)/shard_map/reduce_sum | solution.py:43
  297.4 5.6 %psum.7 = f32[512]{0:T(512)} all-reduce(f32[512]{0:T(512)S(1)} %get-tuple-element.2), channel_id=1, replica_groups=mesh['expert'=16,'tensor'=2] {'tensor'}, use_global_device_ids=true, to_apply=%region_5.6 | all-reduce | flops 512 | bytes 4096 | tf_op jit(solution)/shard_map/psum | solution.py:44
  (5 shorter events, 0.1 us)
Async XLA Ops:
  7.2 16.4 %all-gather.2.cloned.1.call-start = ((), (), s32[]{:S(2)}) async-start(), calls=%async_computation.2 | async-start | bytes 4718592 | tf_op jit(solution)/shard_map/all_gather | solution.py:26
  193.8 92.8 %all-to-all-start.1 = ((bf16[16,64,2048]{2,1,0:T(8,128)(2,1)}), bf16[16,64,2048]{2,1,0:T(8,128)(2,1)}, u32[]{:S(2)}, u32[]{:S(2)}) async-start(bf16[16,64,2048]{2,1,0:T(8,128)(2,1)} %fusion.4), calls=%async_computation.1 | async-start | bytes 8388608 | tf_op jit(solution)/shard_map/all_to_all | solution.py:33
  286.6 7.2 %copy-start = (f32[512]{0:T(512)S(1)}, f32[512]{0:T(512)}, u32[]{:S(2)}) copy-start(f32[512]{0:T(512)} %param.7) | copy-start | bytes 6148
Sparse Core Ops, SparseCore 0:
  9.5 13.9 all-gather.1
where the time goes:
time: 314 us; the launch traced here: 310 us
  blocking collectives  149 us (47%)
  waiting for transfers between devices  98.6 us (31%)
  local copies, waits for them, and re-layouts  18.7 us (6%)
  matrix products  17.5 us (6%)
  between operations  14.1 us (4%)
  other arithmetic  7.01 us (2%)
  starting transfers between devices  4.6 us (1%)
    all_to_all x1, blocking collectives, body(): lax.all_to_all(send, 'expert', split_axis=0, concat_axis=0, tiled=True)  144 us
    all_to_all x1, waiting for transfers between devices, body(): lax.all_to_all(product.astype(jnp.bfloat16).reshape(experts, slots, w_dow...  88.2 us
    dot_general x1, matrix products, body(): jnp.einsum('sxcd,xfd->sxcf', shaped, w_down, preferred_element_type=jnp.f...  17.5 us
    all_gather x1, waiting for transfers between devices, body(): outgoing = lax.all_gather(grad_out, 'tensor', axis=1, tiled=True)  9.67 us
    gather x1, local copies, waits for them, and re-layouts, body(): returned = flat[target].astype(jnp.float32)  7.15 us
    gather x1, local copies, waits for them, and re-layouts, body(): send = padded[source].reshape(experts, capacity, outgoing.shape[1])  6.78 us
  transfers between devices with their start and end apart: 2, of which 2 were waited for; matrix products, arithmetic and copies ran while one was open for 2% of the time, Pallas kernels for 0%

commit v1 on v0

v1 whole, which is shorter than its diff:
```python
import functools

import jax
import jax.numpy as jnp
from jax import lax
from jax.experimental import pallas as pl
from jax.experimental.pallas import tpu as pltpu
from jax.sharding import PartitionSpec as P

MESH = pl.DeviceIdType.MESH
LANES = 128


def across(index, step, count):
    total, bit = 0, 1
    while bit < count:
        total = total + lax.rem(lax.div(index, bit) + lax.div(step, bit), 2) * bit
        bit *= 2
    return total


def steps_of(pair, groups):
    quarter = groups // 4
    near = jnp.where(pair < quarter, quarter + pair, lax.rem(pair + 1, quarter))
    return groups // 2 + pair, near


def tiled_lanes(column, width):
    return jnp.concatenate([column] * (width // LANES), axis=1)


def kernel(
    groups,
    parts,
    capacity,
    tile,
    grad_ref,
    hidden_ref,
    gate_ref,
    ids_ref,
    w_ref,
    out_ref,
    gate_out_ref,
    grad,
    hidden,
    weight,
    outgoing,
    arrived,
    product,
    returned,
    total,
    slot_row,
    slot_column,
    gate_column,
    sums,
    gate_sums,
    local_sem,
    send_sem,
    recv_sem,
    peer_send_sem,
    peer_recv_sem,
    back_send_sem,
    back_recv_sem,
    gate_send_sem,
    gate_recv_sem,
):
    me = lax.axis_index("expert")
    part = lax.axis_index("tensor")
    pairs = groups // 2
    both = 2 * capacity
    tokens, width = grad.shape
    units = weight.shape[0]

    load_grad = pltpu.make_async_copy(grad_ref, grad, local_sem.at[0])
    load_weight = pltpu.make_async_copy(w_ref, weight, local_sem.at[1])
    load_hidden = pltpu.make_async_copy(hidden_ref, hidden, local_sem.at[2])
    load_grad.start()
    load_weight.start()
    load_hidden.start()

    barrier = pltpu.get_barrier_semaphore()

    @pl.loop(1, groups)
    def _(step):
        pl.semaphore_signal(
            barrier, inc=1, device_id=(across(me, step, groups), part), device_id_type=MESH
        )

    for hop in range(1, parts):
        pl.semaphore_signal(
            barrier, inc=1, device_id=(me, lax.rem(part + hop, parts)), device_id_type=MESH
        )

    ids = ids_ref[...]
    ids_column = jnp.broadcast_to(ids, (LANES, tokens)).T
    earlier = jnp.zeros((1, tokens), jnp.int32)
    for start in range(0, tokens, LANES):
        rows = min(LANES, tokens - start)
        shape = (rows, tokens)
        same = tiled_lanes(ids_column[start : start + rows], tokens) == ids
        before = lax.broadcasted_iota(jnp.int32, shape, 0) + start < lax.broadcasted_iota(
            jnp.int32, shape, 1
        )
        earlier = earlier + jnp.sum(
            jnp.where(same & before, 1, 0), axis=0, keepdims=True
        )
    slots = ids * capacity + earlier
    slot_row[...] = slots
    slot_column[...] = jnp.broadcast_to(slots, (LANES, tokens)).T
    gate_column[...] = jnp.broadcast_to(gate_ref[...], (LANES, tokens)).T

    load_grad.wait()

    def rows_of(pair):
        return pl.ds(pl.multiple_of(pair * both, both), both)

    def rows_at(slot):
        return pl.ds(pl.multiple_of(slot * capacity, capacity), capacity)

    def pack(pair, target):
        far, near = steps_of(pair, groups)
        row = lax.broadcasted_iota(jnp.int32, (capacity, tokens), 0)
        chosen = [
            jnp.where(slot_row[...] == row + across(me, step, groups) * capacity, 1.0, 0.0)
            for step in (far, near)
        ]
        pick = jnp.concatenate(chosen, axis=0).astype(jnp.bfloat16)
        rows = jnp.dot(pick, grad[...], preferred_element_type=jnp.float32)
        target[rows_of(pair), :] = rows.astype(jnp.bfloat16)

    def outward(slot, step):
        return pltpu.make_async_remote_copy(
            src_ref=outgoing.at[rows_at(slot)],
            dst_ref=arrived.at[part, rows_at(slot)],
            send_sem=send_sem.at[slot],
            recv_sem=recv_sem.at[slot],
            device_id=(across(me, step, groups), part),
            device_id_type=MESH,
        )

    def sideways(pair, hop):
        return pltpu.make_async_remote_copy(
            src_ref=arrived.at[part, rows_of(pair)],
            dst_ref=arrived.at[part, rows_of(pair)],
            send_sem=peer_send_sem.at[hop - 1, pair],
            recv_sem=peer_recv_sem.at[hop - 1, pair],
            device_id=(me, lax.rem(part + hop, parts)),
            device_id_type=MESH,
        )

    def sideways_in(pair, hop):
        sender = lax.rem(part + parts - hop, parts)
        return pltpu.make_async_remote_copy(
            src_ref=arrived.at[sender, rows_of(pair)],
            dst_ref=arrived.at[sender, rows_of(pair)],
            send_sem=peer_send_sem.at[hop - 1, pair],
            recv_sem=peer_recv_sem.at[hop - 1, pair],
            device_id=(me, lax.rem(part + hop, parts)),
            device_id_type=MESH,
        )

    def homeward(slot, step):
        return pltpu.make_async_remote_copy(
            src_ref=product.at[rows_at(slot)],
            dst_ref=returned.at[rows_at(slot)],
            send_sem=back_send_sem.at[slot],
            recv_sem=back_recv_sem.at[slot],
            device_id=(across(me, step, groups), part),
            device_id_type=MESH,
        )

    own = pairs - 1
    own_rows = pl.ds((groups - 1) * capacity, capacity)

    pack(0, outgoing)
    pl.semaphore_wait(barrier, groups - 1 + parts - 1)
    outward(0, groups // 2).start()
    outward(1, steps_of(0, groups)[1]).start()

    @pl.loop(1, pairs)
    def _(pair):
        pack(pair, outgoing)
        far, near = steps_of(pair, groups)
        outward(2 * pair, far).start()

        @pl.when(pair < own)
        def _():
            outward(2 * pair + 1, near).start()

    arrived[part, own_rows, :] = outgoing[own_rows, :]

    def multiply(pair):
        @pl.loop(0, units // tile)
        def _(block):
            columns = pl.ds(pl.multiple_of(block * tile, tile), tile)
            value = jnp.zeros((both, tile), jnp.float32)
            for piece in range(parts):
                value = value + lax.dot_general(
                    arrived[piece, rows_of(pair), :],
                    weight[columns, piece * width : (piece + 1) * width],
                    (((1,), (1,)), ((), ())),
                    preferred_element_type=jnp.float32,
                )
            product[rows_of(pair), columns] = value.astype(jnp.bfloat16)

    @pl.loop(0, pairs + 1)
    def _(turn):
        @pl.when(turn < pairs)
        def _():
            far, near = steps_of(turn, groups)
            outward(2 * turn, far).wait_recv()

            @pl.when(turn < own)
            def _():
                outward(2 * turn + 1, near).wait_recv()

            for hop in range(1, parts):
                sideways(turn, hop).start()

        @pl.when(turn == 0)
        def _():
            load_weight.wait()

        @pl.when(turn > 0)
        def _():
            pair = turn - 1
            for hop in range(1, parts):
                sideways_in(pair, hop).wait_recv()
            multiply(pair)
            far, near = steps_of(pair, groups)
            homeward(2 * pair, far).start()

            @pl.when(pair < own)
            def _():
                homeward(2 * pair + 1, near).start()

    returned[own_rows, :] = product[own_rows, :]
    load_hidden.wait()
    total[...] = jnp.zeros_like(total)
    sums[...] = jnp.zeros_like(sums)

    def placement(pair, rows):
        far, near = steps_of(pair, groups)
        lane = lax.broadcasted_iota(jnp.int32, (1, both), 1)
        wanted = jnp.where(
            lane < capacity,
            lane + across(me, far, groups) * capacity,
            lane + (across(me, near, groups) - 1) * capacity,
        )
        hit = slot_column[rows, :both] == wanted
        return jnp.where(hit, 1.0, 0.0).astype(jnp.bfloat16)

    def wait_home(pair):
        far, near = steps_of(pair, groups)
        homeward(2 * pair, far).wait_recv()

        @pl.when(pair < own)
        def _():
            homeward(2 * pair + 1, near).wait_recv()

    everything = pl.ds(0, tokens)

    @pl.loop(0, own)
    def _(pair):
        wait_home(pair)
        place = placement(pair, everything)

        @pl.loop(0, units // tile)
        def _(block):
            columns = pl.ds(pl.multiple_of(block * tile, tile), tile)
            total[:, columns] += jnp.dot(
                place, returned[rows_of(pair), columns], preferred_element_type=jnp.float32
            )

    wait_home(own)
    chunk = min(LANES, tokens)

    @pl.loop(0, tokens // chunk)
    def _(part_of):
        rows = pl.ds(pl.multiple_of(part_of * chunk, chunk), chunk)
        place = placement(own, rows)
        gate = tiled_lanes(gate_column[rows, :], tile)

        @pl.loop(0, units // tile)
        def _(block):
            columns = pl.ds(pl.multiple_of(block * tile, tile), tile)
            back = total[rows, columns] + jnp.dot(
                place, returned[rows_of(own), columns], preferred_element_type=jnp.float32
            )
            out_ref[rows, columns] = (gate * back).astype(jnp.bfloat16)
            terms = hidden[rows, columns].astype(jnp.float32) * back
            sums[rows, :] += sum(
                terms[:, at : at + LANES] for at in range(0, tile, LANES)
            )

    row = jnp.sum(sums[...].T, axis=0, keepdims=True)
    gate_sums[part] = jnp.broadcast_to(row, (8, tokens))

    def gate_copy(hop, sender):
        return pltpu.make_async_remote_copy(
            src_ref=gate_sums.at[sender],
            dst_ref=gate_sums.at[sender],
            send_sem=gate_send_sem.at[hop - 1],
            recv_sem=gate_recv_sem.at[hop - 1],
            device_id=(me, lax.rem(part + hop, parts)),
            device_id_type=MESH,
        )

    for hop in range(1, parts):
        gate_copy(hop, part).start()

    @pl.loop(0, pairs)
    def _(pair):
        far, near = steps_of(pair, groups)
        outward(2 * pair, far).wait_send()
        homeward(2 * pair, far).wait_send()
        for hop in range(1, parts):
            sideways(pair, hop).wait_send()

        @pl.when(pair < own)
        def _():
            outward(2 * pair + 1, near).wait_send()
            homeward(2 * pair + 1, near).wait_send()

    for hop in range(1, parts):
        gate_copy(hop, part).wait_send()
        gate_copy(hop, lax.rem(part + parts - hop, parts)).wait_recv()
    result = gate_sums[0]
    for piece in range(1, parts):
        result = result + gate_sums[piece]
    gate_out_ref[...] = result[:1]


def body(groups, parts, grad_out, hidden_in, gate_prob, expert_ids, w_down):
    tokens, width = grad_out.shape
    _, units, features = w_down.shape
    capacity = 2 * tokens // (groups * w_down.shape[0])
    tile = min(512, units)
    rows = groups * capacity
    dma = pltpu.SemaphoreType.DMA
    hops = max(parts - 1, 1)
    grad_hidden, grad_gate = pl.pallas_call(
        functools.partial(kernel, groups, parts, capacity, tile),
        out_shape=(
            jax.ShapeDtypeStruct((tokens, units), jnp.bfloat16),
            jax.ShapeDtypeStruct((1, tokens), jnp.float32),
        ),
        in_specs=[
            pl.BlockSpec(memory_space=pl.ANY),
            pl.BlockSpec(memory_space=pl.ANY),
            pl.BlockSpec(memory_space=pltpu.VMEM),
            pl.BlockSpec(memory_space=pltpu.VMEM),
            pl.BlockSpec(memory_space=pl.ANY),
        ],
        out_specs=(
            pl.BlockSpec(memory_space=pltpu.VMEM),
            pl.BlockSpec(memory_space=pltpu.VMEM),
        ),
        scratch_shapes=[
            pltpu.VMEM((tokens, width), jnp.bfloat16),
            pltpu.VMEM((tokens, units), jnp.bfloat16),
            pltpu.VMEM((units, features), jnp.bfloat16),
            pltpu.VMEM((rows, width), jnp.bfloat16),
            pltpu.VMEM((parts, rows, width), jnp.bfloat16),
            pltpu.VMEM((rows, units), jnp.bfloat16),
            pltpu.VMEM((rows, units), jnp.bfloat16),
            pltpu.VMEM((tokens, units), jnp.float32),
            pltpu.VMEM((1, tokens), jnp.int32),
            pltpu.VMEM((tokens, LANES), jnp.int32),
            pltpu.VMEM((tokens, LANES), jnp.float32),
            pltpu.VMEM((tokens, LANES), jnp.float32),
            pltpu.VMEM((parts, 8, tokens), jnp.float32),
            dma((3,)),
            dma((groups,)),
            dma((groups,)),
            dma((hops, groups // 2)),
            dma((hops, groups // 2)),
            dma((groups,)),
            dma((groups,)),
            dma((hops,)),
            dma((hops,)),
        ],
        compiler_params=pltpu.CompilerParams(
            collective_id=0, has_side_effects=True, vmem_limit_bytes=56 * 1024 * 1024
        ),
    )(
        grad_out,
        hidden_in,
        gate_prob.reshape(1, tokens),
        expert_ids.reshape(1, tokens),
        w_down.reshape(units, features),
    )
    return grad_hidden, grad_gate.reshape(tokens)


def solution(mesh):
    return jax.shard_map(
        functools.partial(body, mesh.shape["expert"], mesh.shape["tensor"]),
        mesh=mesh,
        in_specs=(
            P("expert", "tensor"),
            P("expert", "tensor"),
            P("expert"),
            P("expert", None),
            P("expert", "tensor", None),
        ),
        out_specs=(P("expert", "tensor"), P("expert")),
        check_vma=False,
    )
```

time: 314 us -> 176 us (0.56); the launches traced: 310 us -> 176 us
  Pallas kernels: 0 us -> 171 us
  blocking collectives: 149 us -> 0 us
  waiting for transfers between devices: 98.6 us -> 0 us
  matrix products: 17.5 us -> 0 us
  local copies, waits for them, and re-layouts: 18.7 us -> 3.74 us
  between operations: 14.1 us -> 0.65 us
  other arithmetic: 7.01 us -> 0 us
  starting transfers between devices: 4.6 us -> 0 us
    pallas_call x0 -> x1, Pallas kernels: none -> 171 us  [body(): pl.pallas_call(functools.partial(kernel, groups, parts, capacity, tile),...]
    all_to_all x1 -> x0, blocking collectives: 144 us -> none  [body(): lax.all_to_all(send, 'expert', split_axis=0, concat_axis=0, tiled=True)]
    all_to_all x1 -> x0, waiting for transfers between devices: 88.2 us -> none  [body(): lax.all_to_all(product.astype(jnp.bfloat16).reshape(experts, slots, w_dow...]
    dot_general x1 -> x0, matrix products: 17.5 us -> none  [body(): jnp.einsum('sxcd,xfd->sxcf', shaped, w_down, preferred_element_type=jnp.f...]
    gather x2 -> x0, local copies, waits for them, and re-layouts: 13.9 us -> none  [the longest x1 7.15 us: body(): returned = flat[target].astype(jnp.float32)]
    all_gather x1 -> x0, waiting for transfers between devices: 9.67 us -> none  [body(): outgoing = lax.all_gather(grad_out, 'tensor', axis=1, tiled=True)]
    psum x1 -> x0, blocking collectives: 5.61 us -> none  [body(): grad_gate = lax.psum(partial_sum, 'tensor')]
    all_to_all x1 -> x0, starting transfers between devices: 4.57 us -> none  [body(): lax.all_to_all(product.astype(jnp.bfloat16).reshape(experts, slots, w_dow...]
  transfers between devices with their start and end apart: 2 -> 0, of which waited for: 2 -> 0; matrix products, arithmetic and copies ran while one was open for 2% -> 0% of each run, Pallas kernels for 0% -> 0%
where the time goes in v1:
time: 176 us
  Pallas kernels  171 us (97%)
  local copies, waits for them, and re-layouts  3.74 us (2%)
    pallas_call x1, Pallas kernels, body(): pl.pallas_call(functools.partial(kernel, groups, parts, capacity, tile),...  171 us
    unnamed x4, local copies, waits for them, and re-layouts  3.74 us

profile of v1, /device:TPU:9, one launch (start us, length us, event | category | flops | bytes accessed | tf_op | source)
XLA Modules:
  0.0 175.8 jit_solution(7782539097802348025)
XLA Ops:
  0.6 171.4 %shard_map.68 = (bf16[512,2048]{1,0:T(8,128)(2,1)}, f32[1,512]{1,0:T(1,128)}) custom-call(bf16[512,1536]{1,0:T(8,128)(2,1)} %grad_ref.1, bf16[512,2048]{1,0:T(8,128)(2,1)} %hidden_ref.1, f32[1,512]{1,0:T(1,128)} %bitcast.5, s32[1,512]{1,0:T(1,128)} %bitcast.6, bf16[2048,3072]{1,0:T(8,128)(2,1)} %bitcast.4), custom_call_target="tpu_custom_call" | custom-call | tf_op jit(solution)/shard_map/pallas_call | solution.py:342
  172.1 0.0 copy-start
  172.1 3.2 %copy.9 = bf16[512,2048]{1,0:T(8,128)(2,1)} copy(bf16[512,2048]{1,0:T(8,128)(2,1)} %get-tuple-element.8) | data formatting | bytes 4194304
  175.2 0.0 copy-done
  175.2 0.6 copy.10
Async XLA Ops:
  172.1 3.2 %copy-start = (f32[1,512]{1,0:T(1,128)S(1)}, f32[1,512]{1,0:T(1,128)}, u32[]{:S(2)}) copy-start(f32[1,512]{1,0:T(1,128)} %get-tuple-element.5) | copy-start | bytes 6148

commit v2 on v1

--- a/solution.py
+++ b/solution.py
@@ -9,6 +9,7 @@
 
 MESH = pl.DeviceIdType.MESH
 LANES = 128
+FAR = "far"
 
 
 def across(index, step, count):
@@ -34,13 +35,14 @@
     parts,
     capacity,
     tile,
+    spill,
     grad_ref,
     hidden_ref,
-    gate_ref,
     ids_ref,
     w_ref,
     out_ref,
     gate_out_ref,
+    most_ref,
     grad,
     hidden,
     weight,
@@ -51,7 +53,6 @@
     total,
     slot_row,
     slot_column,
-    gate_column,
     sums,
     gate_sums,
     local_sem,
@@ -63,6 +64,7 @@
     back_recv_sem,
     gate_send_sem,
     gate_recv_sem,
+    *spill_refs,
 ):
     me = lax.axis_index("expert")
     part = lax.axis_index("tensor")
@@ -70,6 +72,34 @@
     both = 2 * capacity
     tokens, width = grad.shape
     units = weight.shape[0]
+    middle = groups // 2
+    half = capacity // 2
+    side = lax.div(me, middle)
+    local = me - side * middle
+    if spill:
+        (
+            spill_column,
+            place_out,
+            place_in,
+            counts,
+            spill_out,
+            spill_in,
+            relay_out,
+            relay_back,
+            spill_back,
+            spill_home,
+            place_sem,
+            count_send_sem,
+            count_recv_sem,
+            spill_sem,
+            relay_send_sem,
+            relay_recv_sem,
+            relay_back_send_sem,
+            relay_back_recv_sem,
+            spill_back_sem,
+        ) = spill_refs
+        lanes = place_in.shape[1]
+    far_rows = half if spill else capacity
 
     load_grad = pltpu.make_async_copy(grad_ref, grad, local_sem.at[0])
     load_weight = pltpu.make_async_copy(w_ref, weight, local_sem.at[1])
@@ -107,15 +137,46 @@
     slots = ids * capacity + earlier
     slot_row[...] = slots
     slot_column[...] = jnp.broadcast_to(slots, (LANES, tokens)).T
-    gate_column[...] = jnp.broadcast_to(gate_ref[...], (LANES, tokens)).T
+    if spill:
+        expert_side = jnp.where(ids >= middle, 1, 0)
+        over = jnp.where((expert_side != side) & (earlier >= half), 1, 0)
+        over_column = jnp.broadcast_to(over, (LANES, tokens)).T
+        order = jnp.zeros((1, tokens), jnp.int32)
+        for start in range(0, tokens, LANES):
+            rows = min(LANES, tokens - start)
+            shape = (rows, tokens)
+            before = lax.broadcasted_iota(jnp.int32, shape, 0) + start < lax.broadcasted_iota(
+                jnp.int32, shape, 1
+            )
+            ahead = tiled_lanes(over_column[start : start + rows], tokens)
+            order = order + jnp.sum(jnp.where(before, ahead, 0), axis=0, keepdims=True)
+        order = jnp.where(over > 0, order, -1)
+        spill_column[...] = jnp.broadcast_to(order, (LANES, tokens)).T
+        spot = (ids - expert_side * middle) * half + earlier - half + 1
+        spot_column = jnp.broadcast_to(spot, (LANES, tokens)).T
+        match = tiled_lanes(spill_column[...], lanes) == lax.broadcasted_iota(
+            jnp.int32, (tokens, lanes), 1
+        )
+        place_out[...] = (
+            jnp.sum(
+                jnp.where(match, tiled_lanes(spot_column, lanes), 0), axis=0, keepdims=True
+            )
+            - 1
+        )
+        counts[0] = jnp.broadcast_to(jnp.sum(over, axis=1, keepdims=True), (1, LANES))
+        spill_in[spill:, :] = jnp.zeros((lanes - spill, width), jnp.bfloat16)
+        spill_home[spill:, :] = jnp.zeros((lanes - spill, units), jnp.bfloat16)
+
+        @pl.loop(0, pairs)
+        def _(pair):
+            unused = pl.ds(pl.multiple_of(pair * both + half, half), half)
+            returned[unused, :] = jnp.zeros((half, units), jnp.bfloat16)
+
 
     load_grad.wait()
 
     def rows_of(pair):
         return pl.ds(pl.multiple_of(pair * both, both), both)
-
-    def rows_at(slot):
-        return pl.ds(pl.multiple_of(slot * capacity, capacity), capacity)
 
     def pack(pair, target):
         far, near = steps_of(pair, groups)
@@ -128,10 +189,14 @@
         rows = jnp.dot(pick, grad[...], preferred_element_type=jnp.float32)
         target[rows_of(pair), :] = rows.astype(jnp.bfloat16)
 
-    def outward(slot, step):
+    def sent_rows(slot, step):
+        size = far_rows if step is FAR else capacity
+        return pl.ds(pl.multiple_of(slot * capacity, capacity), size)
+
+    def outward(slot, step, kind=None):
         return pltpu.make_async_remote_copy(
-            src_ref=outgoing.at[rows_at(slot)],
-            dst_ref=arrived.at[part, rows_at(slot)],
+            src_ref=outgoing.at[sent_rows(slot, kind)],
+            dst_ref=arrived.at[part, sent_rows(slot, kind)],
             send_sem=send_sem.at[slot],
             recv_sem=recv_sem.at[slot],
             device_id=(across(me, step, groups), part),
@@ -159,10 +224,10 @@
             device_id_type=MESH,
         )
 
-    def homeward(slot, step):
+    def homeward(slot, step, kind=None):
         return pltpu.make_async_remote_copy(
-            src_ref=product.at[rows_at(slot)],
-            dst_ref=returned.at[rows_at(slot)],
+            src_ref=product.at[sent_rows(slot, kind)],
+            dst_ref=returned.at[sent_rows(slot, kind)],
             send_sem=back_send_sem.at[slot],
             recv_sem=back_recv_sem.at[slot],
             device_id=(across(me, step, groups), part),
@@ -172,20 +237,127 @@
     own = pairs - 1
     own_rows = pl.ds((groups - 1) * capacity, capacity)
 
-    pack(0, outgoing)
-    pl.semaphore_wait(barrier, groups - 1 + parts - 1)
-    outward(0, groups // 2).start()
-    outward(1, steps_of(0, groups)[1]).start()
-
-    @pl.loop(1, pairs)
-    def _(pair):
-        pack(pair, outgoing)
+    def send_pair(pair):
         far, near = steps_of(pair, groups)
-        outward(2 * pair, far).start()
+        outward(2 * pair, far, FAR).start()
 
         @pl.when(pair < own)
         def _():
             outward(2 * pair + 1, near).start()
+
+    if spill:
+        mirror = (across(me, middle, groups), part)
+
+        def to_mirror(source, target, sems):
+            return pltpu.make_async_remote_copy(
+                src_ref=source,
+                dst_ref=target,
+                send_sem=sems.at[0],
+                recv_sem=sems.at[1],
+                device_id=mirror,
+                device_id_type=MESH,
+            )
+
+        def send_count(step):
+            return pltpu.make_async_remote_copy(
+                src_ref=counts.at[0],
+                dst_ref=counts.at[step],
+                send_sem=count_send_sem.at[step],
+                recv_sem=count_recv_sem.at[step],
+                device_id=(across(me, step, groups), part),
+                device_id_type=MESH,
+            )
+
+        def half_rows(index):
+            return pl.ds(pl.multiple_of(index * half, half), half)
+
+        def second_half(pair):
+            return pl.ds(pl.multiple_of(pair * both + half, half), half)
+
+        def relay(step):
+            target = across(me, step, groups)
+            return pltpu.make_async_remote_copy(
+                src_ref=relay_out.at[half_rows(target - side * middle)],
+                dst_ref=arrived.at[part, second_half(step)],
+                send_sem=relay_send_sem.at[step],
+                recv_sem=relay_recv_sem.at[step],
+                device_id=(target, part),
+                device_id_type=MESH,
+            )
+
+        def relay_home(step):
+            return pltpu.make_async_remote_copy(
+                src_ref=product.at[second_half(step)],
+                dst_ref=relay_back.at[half_rows(local)],
+                send_sem=relay_back_send_sem.at[step],
+                recv_sem=relay_back_recv_sem.at[step],
+                device_id=(across(me, step, groups), part),
+                device_id_type=MESH,
+            )
+
+        def relay_home_in(step):
+            sender = across(me, step, groups) - side * middle
+            return pltpu.make_async_remote_copy(
+                src_ref=product.at[second_half(step)],
+                dst_ref=relay_back.at[half_rows(sender)],
+                send_sem=relay_back_send_sem.at[step],
+                recv_sem=relay_back_recv_sem.at[step],
+                device_id=(across(me, step, groups), part),
+                device_id_type=MESH,
+            )
+
+        place_copy = to_mirror(place_out, place_in, place_sem)
+        spill_copy = to_mirror(spill_out, spill_in.at[pl.ds(0, spill)], spill_sem)
+        spill_back_copy = to_mirror(
+            spill_back, spill_home.at[pl.ds(0, spill)], spill_back_sem
+        )
+        index = lax.broadcasted_iota(jnp.int32, (spill, tokens), 0)
+        pick = jnp.where(order == index, 1.0, 0.0).astype(jnp.bfloat16)
+        spill_out[...] = jnp.dot(
+            pick, grad[...], preferred_element_type=jnp.float32
+        ).astype(jnp.bfloat16)
+        pl.semaphore_wait(barrier, groups - 1 + parts - 1)
+        place_copy.start()
+        spill_copy.start()
+        early = pairs // 2
+
+        @pl.loop(0, early)
+        def _(pair):
+            pack(pair, outgoing)
+            send_pair(pair)
+
+        place_copy.wait_recv()
+        spill_copy.wait_recv()
+        index = lax.broadcasted_iota(jnp.int32, (middle * half, lanes), 0)
+        pick = jnp.where(place_in[...] == index, 1.0, 0.0).astype(jnp.bfloat16)
+        relay_out[...] = jnp.dot(
+            pick, spill_in[...], preferred_element_type=jnp.float32
+        ).astype(jnp.bfloat16)
+
+        @pl.loop(1, middle)
+        def _(step):
+            relay(step).start()
+
+        arrived[part, half:capacity, :] = relay_out[half_rows(local), :]
+
+        @pl.loop(early, pairs)
+        def _(pair):
+            pack(pair, outgoing)
+            send_pair(pair)
+
+        @pl.loop(1, groups)
+        def _(step):
+            send_count(step).start()
+
+    else:
+        pack(0, outgoing)
+        pl.semaphore_wait(barrier, groups - 1 + parts - 1)
+        send_pair(0)
+
+        @pl.loop(1, pairs)
+        def _(pair):
+            pack(pair, outgoing)
+            send_pair(pair)
 
     arrived[part, own_rows, :] = outgoing[own_rows, :]
 
@@ -208,11 +380,17 @@
         @pl.when(turn < pairs)
         def _():
             far, near = steps_of(turn, groups)
-            outward(2 * turn, far).wait_recv()
+            outward(2 * turn, far, FAR).wait_recv()
 
             @pl.when(turn < own)
             def _():
                 outward(2 * turn + 1, near).wait_recv()
+
+            if spill:
+
+                @pl.when(turn > 0)
+                def _():
+                    relay(turn).wait_recv()
 
             for hop in range(1, parts):
                 sideways(turn, hop).start()
@@ -228,11 +406,38 @@
                 sideways_in(pair, hop).wait_recv()
             multiply(pair)
             far, near = steps_of(pair, groups)
-            homeward(2 * pair, far).start()
+            if spill:
+
+                @pl.when(pair > 0)
+                def _():
+                    relay_home(pair).start()
+
+            homeward(2 * pair, far, FAR).start()
 
             @pl.when(pair < own)
             def _():
                 homeward(2 * pair + 1, near).start()
+
+    if spill:
+        relay_back[half_rows(local), :] = product[half:capacity, :]
+
+        @pl.loop(1, middle)
+        def _(step):
+            relay_home_in(step).wait_recv()
+
+        column = jnp.broadcast_to(place_in[...], (LANES, lanes)).T[:spill]
+        index = lax.broadcasted_iota(jnp.int32, (spill, middle * half), 1)
+        wide = jnp.concatenate([column] * -(-middle * half // LANES), axis=1)
+        pick = jnp.where(wide[:, : middle * half] == index, 1.0, 0.0).astype(jnp.bfloat16)
+
+        @pl.loop(0, units // tile)
+        def _(block):
+            columns = pl.ds(pl.multiple_of(block * tile, tile), tile)
+            spill_back[:, columns] = jnp.dot(
+                pick, relay_back[:, columns], preferred_element_type=jnp.float32
+            ).astype(jnp.bfloat16)
+
+        spill_back_copy.start()
 
     returned[own_rows, :] = product[own_rows, :]
     load_hidden.wait()
@@ -247,12 +452,14 @@
             lane + across(me, far, groups) * capacity,
             lane + (across(me, near, groups) - 1) * capacity,
         )
+        if spill:
+            wanted = jnp.where((lane >= half) & (lane < capacity), -1, wanted)
         hit = slot_column[rows, :both] == wanted
         return jnp.where(hit, 1.0, 0.0).astype(jnp.bfloat16)
 
     def wait_home(pair):
         far, near = steps_of(pair, groups)
-        homeward(2 * pair, far).wait_recv()
+        homeward(2 * pair, far, FAR).wait_recv()
 
         @pl.when(pair < own)
         def _():
@@ -260,7 +467,7 @@
 
     everything = pl.ds(0, tokens)
 
-    @pl.loop(0, own)
+    @pl.loop(0, pairs if spill else own)
     def _(pair):
         wait_home(pair)
         place = placement(pair, everything)
@@ -272,22 +479,30 @@
                 place, returned[rows_of(pair), columns], preferred_element_type=jnp.float32
             )
 
-    wait_home(own)
+    if spill:
+        spill_back_copy.wait_recv()
+    else:
+        wait_home(own)
     chunk = min(LANES, tokens)
 
     @pl.loop(0, tokens // chunk)
     def _(part_of):
         rows = pl.ds(pl.multiple_of(part_of * chunk, chunk), chunk)
-        place = placement(own, rows)
-        gate = tiled_lanes(gate_column[rows, :], tile)
+        if spill:
+            lane = lax.broadcasted_iota(jnp.int32, (chunk, lanes), 1)
+            hit = tiled_lanes(spill_column[rows, :], lanes) == lane
+            place = jnp.where(hit, 1.0, 0.0).astype(jnp.bfloat16)
+        else:
+            place = placement(own, rows)
 
         @pl.loop(0, units // tile)
         def _(block):
             columns = pl.ds(pl.multiple_of(block * tile, tile), tile)
+            last = spill_home[:, columns] if spill else returned[rows_of(own), columns]
             back = total[rows, columns] + jnp.dot(
-                place, returned[rows_of(own), columns], preferred_element_type=jnp.float32
-            )
-            out_ref[rows, columns] = (gate * back).astype(jnp.bfloat16)
+                place, last, preferred_element_type=jnp.float32
+            )
+            out_ref[rows, columns] = back.astype(jnp.bfloat16)
             terms = hidden[rows, columns].astype(jnp.float32) * back
             sums[rows, :] += sum(
                 terms[:, at : at + LANES] for at in range(0, tile, LANES)
@@ -312,8 +527,8 @@
     @pl.loop(0, pairs)
     def _(pair):
         far, near = steps_of(pair, groups)
-        outward(2 * pair, far).wait_send()
-        homeward(2 * pair, far).wait_send()
+        outward(2 * pair, far, FAR).wait_send()
+        homeward(2 * pair, far, FAR).wait_send()
         for hop in range(1, parts):
             sideways(pair, hop).wait_send()
 
@@ -322,6 +537,23 @@
             outward(2 * pair + 1, near).wait_send()
             homeward(2 * pair + 1, near).wait_send()
 
+    if spill:
+        place_copy.wait_send()
+        spill_copy.wait_send()
+        spill_back_copy.wait_send()
+
+        @pl.loop(1, middle)
+        def _(step):
+            relay(step).wait_send()
+            relay_home(step).wait_send()
+
+        @pl.loop(1, groups)
+        def _(step):
+            send_count(step).wait()
+
+        most_ref[...] = jnp.max(counts[...], axis=0)
+    else:
+        most_ref[...] = jnp.zeros_like(most_ref)
     for hop in range(1, parts):
         gate_copy(hop, part).wait_send()
         gate_copy(hop, lax.rem(part + parts - hop, parts)).wait_recv()
@@ -331,31 +563,51 @@
     gate_out_ref[...] = result[:1]
 
 
-def body(groups, parts, grad_out, hidden_in, gate_prob, expert_ids, w_down):
+def call(groups, parts, capacity, spill, grad_out, hidden_in, ids, w_down):
     tokens, width = grad_out.shape
-    _, units, features = w_down.shape
-    capacity = 2 * tokens // (groups * w_down.shape[0])
+    units, features = w_down.shape
     tile = min(512, units)
     rows = groups * capacity
     dma = pltpu.SemaphoreType.DMA
     hops = max(parts - 1, 1)
-    grad_hidden, grad_gate = pl.pallas_call(
-        functools.partial(kernel, groups, parts, capacity, tile),
+    middle = groups // 2
+    lanes = -(-spill // LANES) * LANES
+    relayed = middle * capacity // 2
+    spill_scratch = [
+        pltpu.VMEM((tokens, LANES), jnp.int32),
+        pltpu.VMEM((1, lanes), jnp.int32),
+        pltpu.VMEM((1, lanes), jnp.int32),
+        pltpu.VMEM((groups, 1, LANES), jnp.int32),
+        pltpu.VMEM((spill, width), jnp.bfloat16),
+        pltpu.VMEM((lanes, width), jnp.bfloat16),
+        pltpu.VMEM((relayed, width), jnp.bfloat16),
+        pltpu.VMEM((relayed, units), jnp.bfloat16),
+        pltpu.VMEM((spill, units), jnp.bfloat16),
+        pltpu.VMEM((lanes, units), jnp.bfloat16),
+        dma((2,)),
+        dma((groups,)),
+        dma((groups,)),
+        dma((2,)),
+        dma((middle,)),
+        dma((middle,)),
+        dma((middle,)),
+        dma((middle,)),
+        dma((2,)),
+    ]
+    return pl.pallas_call(
+        functools.partial(kernel, groups, parts, capacity, tile, spill),
         out_shape=(
             jax.ShapeDtypeStruct((tokens, units), jnp.bfloat16),
             jax.ShapeDtypeStruct((1, tokens), jnp.float32),
+            jax.ShapeDtypeStruct((1, LANES), jnp.int32),
         ),
         in_specs=[
             pl.BlockSpec(memory_space=pl.ANY),
             pl.BlockSpec(memory_space=pl.ANY),
             pl.BlockSpec(memory_space=pltpu.VMEM),
-            pl.BlockSpec(memory_space=pltpu.VMEM),
             pl.BlockSpec(memory_space=pl.ANY),
         ],
-        out_specs=(
-            pl.BlockSpec(memory_space=pltpu.VMEM),
-            pl.BlockSpec(memory_space=pltpu.VMEM),
-        ),
+        out_specs=(pl.BlockSpec(memory_space=pltpu.VMEM),) * 3,
         scratch_shapes=[
             pltpu.VMEM((tokens, width), jnp.bfloat16),
             pltpu.VMEM((tokens, units), jnp.bfloat16),
@@ -368,7 +620,6 @@
             pltpu.VMEM((1, tokens), jnp.int32),
             pltpu.VMEM((tokens, LANES), jnp.int32),
             pltpu.VMEM((tokens, LANES), jnp.float32),
-            pltpu.VMEM((tokens, LANES), jnp.float32),
             pltpu.VMEM((parts, 8, tokens), jnp.float32),
             dma((3,)),
             dma((groups,)),
@@ -379,18 +630,36 @@
             dma((groups,)),
             dma((hops,)),
             dma((hops,)),
-        ],
+        ]
+        + (spill_scratch if spill else []),
         compiler_params=pltpu.CompilerParams(
-            collective_id=0, has_side_effects=True, vmem_limit_bytes=56 * 1024 * 1024
+            collective_id=1 if spill else 0,
+            has_side_effects=True,
+            vmem_limit_bytes=56 * 1024 * 1024,
         ),
-    )(
-        grad_out,
-        hidden_in,
-        gate_prob.reshape(1, tokens),
-        expert_ids.reshape(1, tokens),
-        w_down.reshape(units, features),
-    )
-    return grad_hidden, grad_gate.reshape(tokens)
+    )(grad_out, hidden_in, ids, w_down)
+
+
+def body(groups, parts, grad_out, hidden_in, gate_prob, expert_ids, w_down):
+    tokens = grad_out.shape[0]
+    experts, units, features = w_down.shape
+    capacity = 2 * tokens // (groups * experts)
+    args = (grad_out, hidden_in, expert_ids.reshape(1, tokens), w_down.reshape(units, features))
+    whole = functools.partial(call, groups, parts, capacity, 0)
+    spill = 9 * groups * capacity // 64 // 16 * 16
+    if capacity % 32 == 0:
+        back, gate_sum, most = call(groups, parts, capacity, spill, *args)
+        back, gate_sum = lax.cond(
+            most[0, 0] > spill,
+            lambda back, gate_sum: whole(*args)[:2],
+            lambda back, gate_sum: (back, gate_sum),
+            back,
+            gate_sum,
+        )
+    else:
+        back, gate_sum, _ = whole(*args)
+    grad_hidden = (gate_prob[:, None] * back.astype(jnp.float32)).astype(jnp.bfloat16)
+    return grad_hidden, gate_sum.reshape(tokens)
 
 
 def solution(mesh):

time: 176 us -> 168 us (0.955)
  the two profiles are of different devices: /device:TPU:9 before, /device:TPU:0 now
where the time goes in v2:
time: 168 us; the launch traced here: 167 us
  Pallas kernels  163 us (97%)
  other arithmetic  1.72 us (1%)
    pallas_call x1, Pallas kernels, call(): pl.pallas_call(functools.partial(kernel, groups, parts, capacity, tile, s...  163 us

profile of v2, /device:TPU:0, one launch (start us, length us, event | category | flops | bytes accessed | tf_op | source)
XLA Modules:
  0.0 167.4 jit_solution(13679807985700047660)
XLA Ops:
  0.6 0.0 copy-start
  0.6 0.0 copy-start.1
  0.6 0.0 copy-start.2
  0.7 163.1 %shard_map.68 = (bf16[512,2048]{1,0:T(8,128)(2,1)S(1)}, f32[1,512]{1,0:T(1,128)S(1)}, s32[1,128]{1,0:T(1,128)}) custom-call(bf16[512,1536]{1,0:T(8,128)(2,1)} %grad_ref.1, bf16[512,2048]{1,0:T(8,128)(2,1)} %hidden_ref.1, s32[1,512]{1,0:T(1,128)} %bitcast.7, bf16[2048,3072]{1,0:T(8,128)(2,1)} %bitcast.5), custom_call_target="tpu_custom_call" | custom-call | tf_op jit(solution)/shard_map/pallas_call | solution.py:597
  164.4 0.0 copy-done
  164.4 0.0 copy-done.1
  164.4 0.0 copy-done.2
  164.4 0.0 copy-start.3
  164.5 0.7 copy-done.3
  165.1 1.7 %fusion = bf16[512,2048]{1,0:T(8,128)(2,1)} fusion(bf16[512,2048]{1,0:T(8,128)(2,1)S(1)} %get-tuple-element.46, f32[512]{0:T(512)S(1)} %copy-done.3), kind=kLoop, calls=%fused_computation.1 | loop fusion | flops 3145728 | bytes 4196352 | tf_op jit(solution)/shard_map/convert_element_type | solution.py:661
  166.9 0.6 copy.12
  (1 shorter events, 0.0 us)
Async XLA Ops:
  0.6 163.8 %copy-start = (bf16[512,2048]{1,0:T(8,128)(2,1)S(1)}, bf16[512,2048]{1,0:T(8,128)(2,1)}, u32[]{:S(2)}) copy-start(bf16[512,2048]{1,0:T(8,128)(2,1)} %hidden_ref.1) | copy-start | bytes 6291460
  0.6 163.8 %copy-start.1 = (bf16[512,1536]{1,0:T(8,128)(2,1)S(1)}, bf16[512,1536]{1,0:T(8,128)(2,1)}, u32[]{:S(2)}) copy-start(bf16[512,1536]{1,0:T(8,128)(2,1)} %grad_ref.1) | copy-start | bytes 4718596
  0.6 163.8 %copy-start.2 = (s32[512,1]{0,1:T(1,128)S(1)}, s32[512,1]{0,1:T(1,128)}, u32[]{:S(2)}) copy-start(s32[512,1]{0,1:T(1,128)} %param.10) | copy-start | bytes 6148
  164.4 0.7 copy-start.3

commit v3 on v2

--- a/solution.py
+++ b/solution.py
@@ -69,7 +69,6 @@
     me = lax.axis_index("expert")
     part = lax.axis_index("tensor")
     pairs = groups // 2
-    both = 2 * capacity
     tokens, width = grad.shape
     units = weight.shape[0]
     middle = groups // 2
@@ -100,6 +99,8 @@
         ) = spill_refs
         lanes = place_in.shape[1]
     far_rows = half if spill else capacity
+    both = far_rows + capacity
+    relayed = middle * half
 
     load_grad = pltpu.make_async_copy(grad_ref, grad, local_sem.at[0])
     load_weight = pltpu.make_async_copy(w_ref, weight, local_sem.at[1])
@@ -137,7 +138,155 @@
     slots = ids * capacity + earlier
     slot_row[...] = slots
     slot_column[...] = jnp.broadcast_to(slots, (LANES, tokens)).T
+    load_grad.wait()
+
+    def rows_of(pair):
+        return pl.ds(pl.multiple_of(pair * both, 16), both)
+
+    def pack(pair, target):
+        far, near = steps_of(pair, groups)
+        chosen = []
+        for step, size in ((far, far_rows), (near, capacity)):
+            row = lax.broadcasted_iota(jnp.int32, (size, tokens), 0)
+            wanted = row + across(me, step, groups) * capacity
+            chosen.append(jnp.where(slot_row[...] == wanted, 1.0, 0.0))
+        pick = jnp.concatenate(chosen, axis=0).astype(jnp.bfloat16)
+        rows = jnp.dot(pick, grad[...], preferred_element_type=jnp.float32)
+        target[rows_of(pair), :] = rows.astype(jnp.bfloat16)
+
+    def sent_rows(slot, kind):
+        pair = lax.div(slot, 2)
+        if kind is FAR:
+            return pl.ds(pl.multiple_of(pair * both, 16), far_rows)
+        return pl.ds(pl.multiple_of(pair * both + far_rows, 16), capacity)
+
+    def outward(slot, step, kind=None):
+        return pltpu.make_async_remote_copy(
+            src_ref=outgoing.at[sent_rows(slot, kind)],
+            dst_ref=arrived.at[part, sent_rows(slot, kind)],
+            send_sem=send_sem.at[slot],
+            recv_sem=recv_sem.at[slot],
+            device_id=(across(me, step, groups), part),
+            device_id_type=MESH,
+        )
+
+    def sideways(pair, hop, rows=None):
+        rows = rows_of(pair) if rows is None else rows
+        return pltpu.make_async_remote_copy(
+            src_ref=arrived.at[part, rows],
+            dst_ref=arrived.at[part, rows],
+            send_sem=peer_send_sem.at[hop - 1, pair],
+            recv_sem=peer_recv_sem.at[hop - 1, pair],
+            device_id=(me, lax.rem(part + hop, parts)),
+            device_id_type=MESH,
+        )
+
+    def sideways_in(pair, hop, rows=None):
+        rows = rows_of(pair) if rows is None else rows
+        sender = lax.rem(part + parts - hop, parts)
+        return pltpu.make_async_remote_copy(
+            src_ref=arrived.at[sender, rows],
+            dst_ref=arrived.at[sender, rows],
+            send_sem=peer_send_sem.at[hop - 1, pair],
+            recv_sem=peer_recv_sem.at[hop - 1, pair],
+            device_id=(me, lax.rem(part + hop, parts)),
+            device_id_type=MESH,
+        )
+
+    def homeward(slot, step, kind=None):
+        return pltpu.make_async_remote_copy(
+            src_ref=product.at[sent_rows(slot, kind)],
+            dst_ref=returned.at[sent_rows(slot, kind)],
+            send_sem=back_send_sem.at[slot],
+            recv_sem=back_recv_sem.at[slot],
+            device_id=(across(me, step, groups), part),
+            device_id_type=MESH,
+        )
+
+    own = pairs - 1
+    own_rows = pl.ds(own * both + far_rows, capacity)
+
+    def send_pair(pair):
+        far, near = steps_of(pair, groups)
+        outward(2 * pair, far, FAR).start()
+
+        @pl.when(pair < own)
+        def _():
+            outward(2 * pair + 1, near).start()
+
     if spill:
+        mirror = (across(me, middle, groups), part)
+
+        def to_mirror(source, target, sems):
+            return pltpu.make_async_remote_copy(
+                src_ref=source,
+                dst_ref=target,
+                send_sem=sems.at[0],
+                recv_sem=sems.at[1],
+                device_id=mirror,
+                device_id_type=MESH,
+            )
+
+        def send_count(step):
+            return pltpu.make_async_remote_copy(
+                src_ref=counts.at[0],
+                dst_ref=counts.at[step],
+                send_sem=count_send_sem.at[step],
+                recv_sem=count_recv_sem.at[step],
+                device_id=(across(me, step, groups), part),
+                device_id_type=MESH,
+            )
+
+        def half_rows(index):
+            return pl.ds(pl.multiple_of(index * half, half), half)
+
+        relay_rows = pl.ds(pairs * both, relayed)
+        own_relay = pl.ds(pairs * both, half)
+
+        def relay_at(step):
+            return pl.ds(pl.multiple_of(pairs * both + step * half, 16), half)
+
+        def relay(step):
+            target = across(me, step, groups)
+            return pltpu.make_async_remote_copy(
+                src_ref=relay_out.at[half_rows(target - side * middle)],
+                dst_ref=arrived.at[part, relay_at(step)],
+                send_sem=relay_send_sem.at[step],
+                recv_sem=relay_recv_sem.at[step],
+                device_id=(target, part),
+                device_id_type=MESH,
+            )
+
+        def relay_home(step):
+            return pltpu.make_async_remote_copy(
+                src_ref=product.at[relay_at(step)],
+                dst_ref=relay_back.at[half_rows(local)],
+                send_sem=relay_back_send_sem.at[step],
+                recv_sem=relay_back_recv_sem.at[step],
+                device_id=(across(me, step, groups), part),
+                device_id_type=MESH,
+            )
+
+        def relay_home_in(step):
+            sender = across(me, step, groups) - side * middle
+            return pltpu.make_async_remote_copy(
+                src_ref=product.at[relay_at(step)],
+                dst_ref=relay_back.at[half_rows(sender)],
+                send_sem=relay_back_send_sem.at[step],
+                recv_sem=relay_back_recv_sem.at[step],
+                device_id=(across(me, step, groups), part),
+                device_id_type=MESH,
+            )
+
+        place_copy = to_mirror(place_out, place_in, place_sem)
+        spill_copy = to_mirror(spill_out, spill_in.at[pl.ds(0, spill)], spill_sem)
+        spill_back_copy = to_mirror(
+            spill_back, spill_home.at[pl.ds(0, spill)], spill_back_sem
+        )
+        early = 3 * pairs // 8
+        pack(0, outgoing)
+        pl.semaphore_wait(barrier, groups - 1 + parts - 1)
+        send_pair(0)
         expert_side = jnp.where(ids >= middle, 1, 0)
         over = jnp.where((expert_side != side) & (earlier >= half), 1, 0)
         over_column = jnp.broadcast_to(over, (LANES, tokens)).T
@@ -166,169 +315,22 @@
         counts[0] = jnp.broadcast_to(jnp.sum(over, axis=1, keepdims=True), (1, LANES))
         spill_in[spill:, :] = jnp.zeros((lanes - spill, width), jnp.bfloat16)
         spill_home[spill:, :] = jnp.zeros((lanes - spill, units), jnp.bfloat16)
-
-        @pl.loop(0, pairs)
-        def _(pair):
-            unused = pl.ds(pl.multiple_of(pair * both + half, half), half)
-            returned[unused, :] = jnp.zeros((half, units), jnp.bfloat16)
-
-
-    load_grad.wait()
-
-    def rows_of(pair):
-        return pl.ds(pl.multiple_of(pair * both, both), both)
-
-    def pack(pair, target):
-        far, near = steps_of(pair, groups)
-        row = lax.broadcasted_iota(jnp.int32, (capacity, tokens), 0)
-        chosen = [
-            jnp.where(slot_row[...] == row + across(me, step, groups) * capacity, 1.0, 0.0)
-            for step in (far, near)
-        ]
-        pick = jnp.concatenate(chosen, axis=0).astype(jnp.bfloat16)
-        rows = jnp.dot(pick, grad[...], preferred_element_type=jnp.float32)
-        target[rows_of(pair), :] = rows.astype(jnp.bfloat16)
-
-    def sent_rows(slot, step):
-        size = far_rows if step is FAR else capacity
-        return pl.ds(pl.multiple_of(slot * capacity, capacity), size)
-
-    def outward(slot, step, kind=None):
-        return pltpu.make_async_remote_copy(
-            src_ref=outgoing.at[sent_rows(slot, kind)],
-            dst_ref=arrived.at[part, sent_rows(slot, kind)],
-            send_sem=send_sem.at[slot],
-            recv_sem=recv_sem.at[slot],
-            device_id=(across(me, step, groups), part),
-            device_id_type=MESH,
-        )
-
-    def sideways(pair, hop):
-        return pltpu.make_async_remote_copy(
-            src_ref=arrived.at[part, rows_of(pair)],
-            dst_ref=arrived.at[part, rows_of(pair)],
-            send_sem=peer_send_sem.at[hop - 1, pair],
-            recv_sem=peer_recv_sem.at[hop - 1, pair],
-            device_id=(me, lax.rem(part + hop, parts)),
-            device_id_type=MESH,
-        )
-
-    def sideways_in(pair, hop):
-        sender = lax.rem(part + parts - hop, parts)
-        return pltpu.make_async_remote_copy(
-            src_ref=arrived.at[sender, rows_of(pair)],
-            dst_ref=arrived.at[sender, rows_of(pair)],
-            send_sem=peer_send_sem.at[hop - 1, pair],
-            recv_sem=peer_recv_sem.at[hop - 1, pair],
-            device_id=(me, lax.rem(part + hop, parts)),
-            device_id_type=MESH,
-        )
-
-    def homeward(slot, step, kind=None):
-        return pltpu.make_async_remote_copy(
-            src_ref=product.at[sent_rows(slot, kind)],
-            dst_ref=returned.at[sent_rows(slot, kind)],
-            send_sem=back_send_sem.at[slot],
-            recv_sem=back_recv_sem.at[slot],
-            device_id=(across(me, step, groups), part),
-            device_id_type=MESH,
-        )
-
-    own = pairs - 1
-    own_rows = pl.ds((groups - 1) * capacity, capacity)
-
-    def send_pair(pair):
-        far, near = steps_of(pair, groups)
-        outward(2 * pair, far, FAR).start()
-
-        @pl.when(pair < own)
-        def _():
-            outward(2 * pair + 1, near).start()
-
-    if spill:
-        mirror = (across(me, middle, groups), part)
-
-        def to_mirror(source, target, sems):
-            return pltpu.make_async_remote_copy(
-                src_ref=source,
-                dst_ref=target,
-                send_sem=sems.at[0],
-                recv_sem=sems.at[1],
-                device_id=mirror,
-                device_id_type=MESH,
-            )
-
-        def send_count(step):
-            return pltpu.make_async_remote_copy(
-                src_ref=counts.at[0],
-                dst_ref=counts.at[step],
-                send_sem=count_send_sem.at[step],
-                recv_sem=count_recv_sem.at[step],
-                device_id=(across(me, step, groups), part),
-                device_id_type=MESH,
-            )
-
-        def half_rows(index):
-            return pl.ds(pl.multiple_of(index * half, half), half)
-
-        def second_half(pair):
-            return pl.ds(pl.multiple_of(pair * both + half, half), half)
-
-        def relay(step):
-            target = across(me, step, groups)
-            return pltpu.make_async_remote_copy(
-                src_ref=relay_out.at[half_rows(target - side * middle)],
-                dst_ref=arrived.at[part, second_half(step)],
-                send_sem=relay_send_sem.at[step],
-                recv_sem=relay_recv_sem.at[step],
-                device_id=(target, part),
-                device_id_type=MESH,
-            )
-
-        def relay_home(step):
-            return pltpu.make_async_remote_copy(
-                src_ref=product.at[second_half(step)],
-                dst_ref=relay_back.at[half_rows(local)],
-                send_sem=relay_back_send_sem.at[step],
-                recv_sem=relay_back_recv_sem.at[step],
-                device_id=(across(me, step, groups), part),
-                device_id_type=MESH,
-            )
-
-        def relay_home_in(step):
-            sender = across(me, step, groups) - side * middle
-            return pltpu.make_async_remote_copy(
-                src_ref=product.at[second_half(step)],
-                dst_ref=relay_back.at[half_rows(sender)],
-                send_sem=relay_back_send_sem.at[step],
-                recv_sem=relay_back_recv_sem.at[step],
-                device_id=(across(me, step, groups), part),
-                device_id_type=MESH,
-            )
-
-        place_copy = to_mirror(place_out, place_in, place_sem)
-        spill_copy = to_mirror(spill_out, spill_in.at[pl.ds(0, spill)], spill_sem)
-        spill_back_copy = to_mirror(
-            spill_back, spill_home.at[pl.ds(0, spill)], spill_back_sem
-        )
         index = lax.broadcasted_iota(jnp.int32, (spill, tokens), 0)
         pick = jnp.where(order == index, 1.0, 0.0).astype(jnp.bfloat16)
         spill_out[...] = jnp.dot(
             pick, grad[...], preferred_element_type=jnp.float32
         ).astype(jnp.bfloat16)
-        pl.semaphore_wait(barrier, groups - 1 + parts - 1)
         place_copy.start()
         spill_copy.start()
-        early = pairs // 2
-
-        @pl.loop(0, early)
+
+        @pl.loop(1, max(early, 1))
         def _(pair):
             pack(pair, outgoing)
             send_pair(pair)
 
         place_copy.wait_recv()
         spill_copy.wait_recv()
-        index = lax.broadcasted_iota(jnp.int32, (middle * half, lanes), 0)
+        index = lax.broadcasted_iota(jnp.int32, (relayed, lanes), 0)
         pick = jnp.where(place_in[...] == index, 1.0, 0.0).astype(jnp.bfloat16)
         relay_out[...] = jnp.dot(
             pick, spill_in[...], preferred_element_type=jnp.float32
@@ -338,9 +340,9 @@
         def _(step):
             relay(step).start()
 
-        arrived[part, half:capacity, :] = relay_out[half_rows(local), :]
-
-        @pl.loop(early, pairs)
+        arrived[part, own_relay, :] = relay_out[half_rows(local), :]
+
+        @pl.loop(max(early, 1), pairs)
         def _(pair):
             pack(pair, outgoing)
             send_pair(pair)
@@ -361,19 +363,57 @@
 
     arrived[part, own_rows, :] = outgoing[own_rows, :]
 
-    def multiply(pair):
+    def multiply(rows):
         @pl.loop(0, units // tile)
         def _(block):
             columns = pl.ds(pl.multiple_of(block * tile, tile), tile)
-            value = jnp.zeros((both, tile), jnp.float32)
+            value = jnp.zeros((rows.size, tile), jnp.float32)
             for piece in range(parts):
                 value = value + lax.dot_general(
-                    arrived[piece, rows_of(pair), :],
+                    arrived[piece, rows, :],
                     weight[columns, piece * width : (piece + 1) * width],
                     (((1,), (1,)), ((), ())),
                     preferred_element_type=jnp.float32,
                 )
-            product[rows_of(pair), columns] = value.astype(jnp.bfloat16)
+            product[rows, columns] = value.astype(jnp.bfloat16)
+
+    if spill:
+
+        def multiply_relayed():
+            @pl.loop(1, middle)
+            def _(step):
+                relay(step).wait_recv()
+
+            for hop in range(1, parts):
+                sideways(pairs, hop, relay_rows).start()
+            for hop in range(1, parts):
+                sideways_in(pairs, hop, relay_rows).wait_recv()
+            multiply(relay_rows)
+
+            @pl.loop(1, middle)
+            def _(step):
+                relay_home(step).start()
+
+        def pack_home():
+            relay_back[half_rows(local), :] = product[own_relay, :]
+
+            @pl.loop(1, middle)
+            def _(step):
+                relay_home_in(step).wait_recv()
+
+            column = jnp.broadcast_to(place_in[...], (LANES, lanes)).T[:spill]
+            index = lax.broadcasted_iota(jnp.int32, (spill, relayed), 1)
+            wide = jnp.concatenate([column] * -(-relayed // LANES), axis=1)
+            pick = jnp.where(wide[:, : relayed] == index, 1.0, 0.0).astype(jnp.bfloat16)
+
+            @pl.loop(0, units // tile)
+            def _(block):
+                columns = pl.ds(pl.multiple_of(block * tile, tile), tile)
+                spill_back[:, columns] = jnp.dot(
+                    pick, relay_back[:, columns], preferred_element_type=jnp.float32
+                ).astype(jnp.bfloat16)
+
+            spill_back_copy.start()
 
     @pl.loop(0, pairs + 1)
     def _(turn):
@@ -386,12 +426,6 @@
             def _():
                 outward(2 * turn + 1, near).wait_recv()
 
-            if spill:
-
-                @pl.when(turn > 0)
-                def _():
-                    relay(turn).wait_recv()
-
             for hop in range(1, parts):
                 sideways(turn, hop).start()
 
@@ -404,40 +438,23 @@
             pair = turn - 1
             for hop in range(1, parts):
                 sideways_in(pair, hop).wait_recv()
-            multiply(pair)
+            multiply(rows_of(pair))
             far, near = steps_of(pair, groups)
-            if spill:
-
-                @pl.when(pair > 0)
-                def _():
-                    relay_home(pair).start()
-
             homeward(2 * pair, far, FAR).start()
 
             @pl.when(pair < own)
             def _():
                 homeward(2 * pair + 1, near).start()
 
-    if spill:
-        relay_back[half_rows(local), :] = product[half:capacity, :]
-
-        @pl.loop(1, middle)
-        def _(step):
-            relay_home_in(step).wait_recv()
-
-        column = jnp.broadcast_to(place_in[...], (LANES, lanes)).T[:spill]
-        index = lax.broadcasted_iota(jnp.int32, (spill, middle * half), 1)
-        wide = jnp.concatenate([column] * -(-middle * half // LANES), axis=1)
-        pick = jnp.where(wide[:, : middle * half] == index, 1.0, 0.0).astype(jnp.bfloat16)
-
-        @pl.loop(0, units // tile)
-        def _(block):
-            columns = pl.ds(pl.multiple_of(block * tile, tile), tile)
-            spill_back[:, columns] = jnp.dot(
-                pick, relay_back[:, columns], preferred_element_type=jnp.float32
-            ).astype(jnp.bfloat16)
-
-        spill_back_copy.start()
+        if spill:
+
+            @pl.when(turn == max(early, 1))
+            def _():
+                multiply_relayed()
+
+            @pl.when(turn == own)
+            def _():
+                pack_home()
 
     returned[own_rows, :] = product[own_rows, :]
     load_hidden.wait()
@@ -448,12 +465,10 @@
         far, near = steps_of(pair, groups)
         lane = lax.broadcasted_iota(jnp.int32, (1, both), 1)
         wanted = jnp.where(
-            lane < capacity,
+            lane < far_rows,
             lane + across(me, far, groups) * capacity,
-            lane + (across(me, near, groups) - 1) * capacity,
-        )
-        if spill:
-            wanted = jnp.where((lane >= half) & (lane < capacity), -1, wanted)
+            lane + across(me, near, groups) * capacity - far_rows,
+        )
         hit = slot_column[rows, :both] == wanted
         return jnp.where(hit, 1.0, 0.0).astype(jnp.bfloat16)
 
@@ -467,40 +482,37 @@
 
     everything = pl.ds(0, tokens)
 
-    @pl.loop(0, pairs if spill else own)
-    def _(pair):
-        wait_home(pair)
-        place = placement(pair, everything)
-
+    def gather(place, source, rows):
         @pl.loop(0, units // tile)
         def _(block):
             columns = pl.ds(pl.multiple_of(block * tile, tile), tile)
             total[:, columns] += jnp.dot(
-                place, returned[rows_of(pair), columns], preferred_element_type=jnp.float32
-            )
+                place, source[rows, columns], preferred_element_type=jnp.float32
+            )
+
+    @pl.loop(0, own)
+    def _(pair):
+        wait_home(pair)
+        gather(placement(pair, everything), returned, rows_of(pair))
 
     if spill:
         spill_back_copy.wait_recv()
-    else:
-        wait_home(own)
+        lane = lax.broadcasted_iota(jnp.int32, (tokens, lanes), 1)
+        hit = tiled_lanes(spill_column[...], lanes) == lane
+        gather(jnp.where(hit, 1.0, 0.0).astype(jnp.bfloat16), spill_home, pl.ds(0, lanes))
+    wait_home(own)
     chunk = min(LANES, tokens)
 
     @pl.loop(0, tokens // chunk)
     def _(part_of):
         rows = pl.ds(pl.multiple_of(part_of * chunk, chunk), chunk)
-        if spill:
-            lane = lax.broadcasted_iota(jnp.int32, (chunk, lanes), 1)
-            hit = tiled_lanes(spill_column[rows, :], lanes) == lane
-            place = jnp.where(hit, 1.0, 0.0).astype(jnp.bfloat16)
-        else:
-            place = placement(own, rows)
+        place = placement(own, rows)
 
         @pl.loop(0, units // tile)
         def _(block):
             columns = pl.ds(pl.multiple_of(block * tile, tile), tile)
-            last = spill_home[:, columns] if spill else returned[rows_of(own), columns]
             back = total[rows, columns] + jnp.dot(
-                place, last, preferred_element_type=jnp.float32
+                place, returned[rows_of(own), columns], preferred_element_type=jnp.float32
             )
             out_ref[rows, columns] = back.astype(jnp.bfloat16)
             terms = hidden[rows, columns].astype(jnp.float32) * back
@@ -538,6 +550,8 @@
             homeward(2 * pair + 1, near).wait_send()
 
     if spill:
+        for hop in range(1, parts):
+            sideways(pairs, hop, relay_rows).wait_send()
         place_copy.wait_send()
         spill_copy.wait_send()
         spill_back_copy.wait_send()
@@ -567,12 +581,13 @@
     tokens, width = grad_out.shape
     units, features = w_down.shape
     tile = min(512, units)
-    rows = groups * capacity
+    rows = groups * capacity * 3 // 4 if spill else groups * capacity
     dma = pltpu.SemaphoreType.DMA
     hops = max(parts - 1, 1)
     middle = groups // 2
     lanes = -(-spill // LANES) * LANES
     relayed = middle * capacity // 2
+    extra = relayed if spill else 0
     spill_scratch = [
         pltpu.VMEM((tokens, LANES), jnp.int32),
         pltpu.VMEM((1, lanes), jnp.int32),
@@ -613,8 +628,8 @@
             pltpu.VMEM((tokens, units), jnp.bfloat16),
             pltpu.VMEM((units, features), jnp.bfloat16),
             pltpu.VMEM((rows, width), jnp.bfloat16),
-            pltpu.VMEM((parts, rows, width), jnp.bfloat16),
-            pltpu.VMEM((rows, units), jnp.bfloat16),
+            pltpu.VMEM((parts, rows + extra, width), jnp.bfloat16),
+            pltpu.VMEM((rows + extra, units), jnp.bfloat16),
             pltpu.VMEM((rows, units), jnp.bfloat16),
             pltpu.VMEM((tokens, units), jnp.float32),
             pltpu.VMEM((1, tokens), jnp.int32),
@@ -624,8 +639,8 @@
             dma((3,)),
             dma((groups,)),
             dma((groups,)),
-            dma((hops, groups // 2)),
-            dma((hops, groups // 2)),
+            dma((hops, groups // 2 + 1)),
+            dma((hops, groups // 2 + 1)),
             dma((groups,)),
             dma((groups,)),
             dma((hops,)),

time: 168 us -> 162 us (0.964)
  the two profiles are of different devices: /device:TPU:0 before, /device:TPU:9 now
where the time goes in v3:
time: 162 us; the launch traced here: 160 us
  Pallas kernels  156 us (96%)
  other arithmetic  1.72 us (1%)
    pallas_call x1, Pallas kernels, call(): pl.pallas_call(functools.partial(kernel, groups, parts, capacity, tile, s...  156 us

profile of v3, /device:TPU:9, one launch (start us, length us, event | category | flops | bytes accessed | tf_op | source)
XLA Modules:
  0.0 160.3 jit_solution(8102719366223270278)
XLA Ops:
  0.6 0.0 copy-start
  0.6 0.0 copy-start.1
  0.6 0.0 copy-start.2
  0.7 155.9 %shard_map.68 = (bf16[512,2048]{1,0:T(8,128)(2,1)S(1)}, f32[1,512]{1,0:T(1,128)S(1)}, s32[1,128]{1,0:T(1,128)}) custom-call(bf16[512,1536]{1,0:T(8,128)(2,1)} %grad_ref.1, bf16[512,2048]{1,0:T(8,128)(2,1)} %hidden_ref.1, s32[1,512]{1,0:T(1,128)} %bitcast.7, bf16[2048,3072]{1,0:T(8,128)(2,1)} %bitcast.5), custom_call_target="tpu_custom_call" | custom-call | tf_op jit(solution)/shard_map/pallas_call | solution.py:612
  157.3 0.0 copy-done
  157.3 0.0 copy-done.1
  157.3 0.0 copy-done.2
  157.3 0.0 copy-start.3
  157.3 0.7 copy-done.3
  158.0 1.7 %fusion = bf16[512,2048]{1,0:T(8,128)(2,1)} fusion(bf16[512,2048]{1,0:T(8,128)(2,1)S(1)} %get-tuple-element.46, f32[512]{0:T(512)S(1)} %copy-done.3), kind=kLoop, calls=%fused_computation.1 | loop fusion | flops 3145728 | bytes 4196352 | tf_op jit(solution)/shard_map/convert_element_type | solution.py:676
  159.7 0.6 copy.12
  (1 shorter events, 0.0 us)
Async XLA Ops:
  0.6 156.7 %copy-start = (bf16[512,2048]{1,0:T(8,128)(2,1)S(1)}, bf16[512,2048]{1,0:T(8,128)(2,1)}, u32[]{:S(2)}) copy-start(bf16[512,2048]{1,0:T(8,128)(2,1)} %hidden_ref.1) | copy-start | bytes 6291460
  0.6 156.7 %copy-start.1 = (bf16[512,1536]{1,0:T(8,128)(2,1)S(1)}, bf16[512,1536]{1,0:T(8,128)(2,1)}, u32[]{:S(2)}) copy-start(bf16[512,1536]{1,0:T(8,128)(2,1)} %grad_ref.1) | copy-start | bytes 4718596
  0.6 156.7 %copy-start.2 = (s32[512,1]{0,1:T(1,128)S(1)}, s32[512,1]{0,1:T(1,128)}, u32[]{:S(2)}) copy-start(s32[512,1]{0,1:T(1,128)} %param.10) | copy-start | bytes 6148
  157.3 0.7 copy-start.3

commit v4 on v3

--- a/solution.py
+++ b/solution.py
@@ -100,6 +100,9 @@
         lanes = place_in.shape[1]
     far_rows = half if spill else capacity
     both = far_rows + capacity
+    span = 2 if pairs % 2 == 0 else 1
+    blocks = pairs // span
+    last = blocks - 1
     relayed = middle * half
 
     load_grad = pltpu.make_async_copy(grad_ref, grad, local_sem.at[0])
@@ -140,19 +143,26 @@
     slot_column[...] = jnp.broadcast_to(slots, (LANES, tokens)).T
     load_grad.wait()
 
-    def rows_of(pair):
-        return pl.ds(pl.multiple_of(pair * both, 16), both)
-
-    def pack(pair, target):
-        far, near = steps_of(pair, groups)
+    def rows_of(block):
+        return pl.ds(pl.multiple_of(block * span * both, 16), span * both)
+
+    def segments(block):
+        found = []
+        for inner in range(span):
+            far, near = steps_of(block * span + inner, groups)
+            found.append((far, inner * both, far_rows))
+            found.append((near, inner * both + far_rows, capacity))
+        return found
+
+    def pack(block, target):
         chosen = []
-        for step, size in ((far, far_rows), (near, capacity)):
+        for step, _, size in segments(block):
             row = lax.broadcasted_iota(jnp.int32, (size, tokens), 0)
             wanted = row + across(me, step, groups) * capacity
             chosen.append(jnp.where(slot_row[...] == wanted, 1.0, 0.0))
         pick = jnp.concatenate(chosen, axis=0).astype(jnp.bfloat16)
         rows = jnp.dot(pick, grad[...], preferred_element_type=jnp.float32)
-        target[rows_of(pair), :] = rows.astype(jnp.bfloat16)
+        target[rows_of(block), :] = rows.astype(jnp.bfloat16)
 
     def sent_rows(slot, kind):
         pair = lax.div(slot, 2)
@@ -170,25 +180,25 @@
             device_id_type=MESH,
         )
 
-    def sideways(pair, hop, rows=None):
-        rows = rows_of(pair) if rows is None else rows
+    def sideways(block, hop, rows=None):
+        rows = rows_of(block) if rows is None else rows
         return pltpu.make_async_remote_copy(
             src_ref=arrived.at[part, rows],
             dst_ref=arrived.at[part, rows],
-            send_sem=peer_send_sem.at[hop - 1, pair],
-            recv_sem=peer_recv_sem.at[hop - 1, pair],
+            send_sem=peer_send_sem.at[hop - 1, block],
+            recv_sem=peer_recv_sem.at[hop - 1, block],
             device_id=(me, lax.rem(part + hop, parts)),
             device_id_type=MESH,
         )
 
-    def sideways_in(pair, hop, rows=None):
-        rows = rows_of(pair) if rows is None else rows
+    def sideways_in(block, hop, rows=None):
+        rows = rows_of(block) if rows is None else rows
         sender = lax.rem(part + parts - hop, parts)
         return pltpu.make_async_remote_copy(
             src_ref=arrived.at[sender, rows],
             dst_ref=arrived.at[sender, rows],
-            send_sem=peer_send_sem.at[hop - 1, pair],
-            recv_sem=peer_recv_sem.at[hop - 1, pair],
+            send_sem=peer_send_sem.at[hop - 1, block],
+            recv_sem=peer_recv_sem.at[hop - 1, block],
             device_id=(me, lax.rem(part + hop, parts)),
             device_id_type=MESH,
         )
@@ -206,13 +216,18 @@
     own = pairs - 1
     own_rows = pl.ds(own * both + far_rows, capacity)
 
-    def send_pair(pair):
-        far, near = steps_of(pair, groups)
-        outward(2 * pair, far, FAR).start()
-
-        @pl.when(pair < own)
-        def _():
-            outward(2 * pair + 1, near).start()
+    def each_pair(block, copy, act):
+        for inner in range(span):
+            pair = block * span + inner
+            far, near = steps_of(pair, groups)
+            act(copy(2 * pair, far, FAR))
+
+            @pl.when(pair < own)
+            def _():
+                act(copy(2 * pair + 1, near))
+
+    def send_block(block):
+        each_pair(block, outward, lambda copy: copy.start())
 
     if spill:
         mirror = (across(me, middle, groups), part)
@@ -283,10 +298,10 @@
         spill_back_copy = to_mirror(
             spill_back, spill_home.at[pl.ds(0, spill)], spill_back_sem
         )
-        early = 3 * pairs // 8
+        early = (blocks + 1) // 2
         pack(0, outgoing)
         pl.semaphore_wait(barrier, groups - 1 + parts - 1)
-        send_pair(0)
+        send_block(0)
         expert_side = jnp.where(ids >= middle, 1, 0)
         over = jnp.where((expert_side != side) & (earlier >= half), 1, 0)
         over_column = jnp.broadcast_to(over, (LANES, tokens)).T
@@ -323,10 +338,10 @@
         place_copy.start()
         spill_copy.start()
 
-        @pl.loop(1, max(early, 1))
-        def _(pair):
-            pack(pair, outgoing)
-            send_pair(pair)
+        @pl.loop(1, early)
+        def _(block):
+            pack(block, outgoing)
+            send_block(block)
 
         place_copy.wait_recv()
         spill_copy.wait_recv()
@@ -342,10 +357,10 @@
 
         arrived[part, own_relay, :] = relay_out[half_rows(local), :]
 
-        @pl.loop(max(early, 1), pairs)
-        def _(pair):
-            pack(pair, outgoing)
-            send_pair(pair)
+        @pl.loop(early, blocks)
+        def _(block):
+            pack(block, outgoing)
+            send_block(block)
 
         @pl.loop(1, groups)
         def _(step):
@@ -354,12 +369,12 @@
     else:
         pack(0, outgoing)
         pl.semaphore_wait(barrier, groups - 1 + parts - 1)
-        send_pair(0)
-
-        @pl.loop(1, pairs)
-        def _(pair):
-            pack(pair, outgoing)
-            send_pair(pair)
+        send_block(0)
+
+        @pl.loop(1, blocks)
+        def _(block):
+            pack(block, outgoing)
+            send_block(block)
 
     arrived[part, own_rows, :] = outgoing[own_rows, :]
 
@@ -385,9 +400,9 @@
                 relay(step).wait_recv()
 
             for hop in range(1, parts):
-                sideways(pairs, hop, relay_rows).start()
+                sideways(blocks, hop, relay_rows).start()
             for hop in range(1, parts):
-                sideways_in(pairs, hop, relay_rows).wait_recv()
+                sideways_in(blocks, hop, relay_rows).wait_recv()
             multiply(relay_rows)
 
             @pl.loop(1, middle)
@@ -415,17 +430,11 @@
 
             spill_back_copy.start()
 
-    @pl.loop(0, pairs + 1)
+    @pl.loop(0, blocks + 1)
     def _(turn):
-        @pl.when(turn < pairs)
+        @pl.when(turn < blocks)
         def _():
-            far, near = steps_of(turn, groups)
-            outward(2 * turn, far, FAR).wait_recv()
-
-            @pl.when(turn < own)
-            def _():
-                outward(2 * turn + 1, near).wait_recv()
-
+            each_pair(turn, outward, lambda copy: copy.wait_recv())
             for hop in range(1, parts):
                 sideways(turn, hop).start()
 
@@ -435,24 +444,18 @@
 
         @pl.when(turn > 0)
         def _():
-            pair = turn - 1
             for hop in range(1, parts):
-                sideways_in(pair, hop).wait_recv()
-            multiply(rows_of(pair))
-            far, near = steps_of(pair, groups)
-            homeward(2 * pair, far, FAR).start()
-
-            @pl.when(pair < own)
-            def _():
-                homeward(2 * pair + 1, near).start()
+                sideways_in(turn - 1, hop).wait_recv()
+            multiply(rows_of(turn - 1))
+            each_pair(turn - 1, homeward, lambda copy: copy.start())
 
         if spill:
 
-            @pl.when(turn == max(early, 1))
+            @pl.when(turn == early)
             def _():
                 multiply_relayed()
 
-            @pl.when(turn == own)
+            @pl.when(turn == max(last, early))
             def _():
                 pack_home()
 
@@ -461,24 +464,18 @@
     total[...] = jnp.zeros_like(total)
     sums[...] = jnp.zeros_like(sums)
 
-    def placement(pair, rows):
-        far, near = steps_of(pair, groups)
-        lane = lax.broadcasted_iota(jnp.int32, (1, both), 1)
-        wanted = jnp.where(
-            lane < far_rows,
-            lane + across(me, far, groups) * capacity,
-            lane + across(me, near, groups) * capacity - far_rows,
-        )
-        hit = slot_column[rows, :both] == wanted
+    def placement(block, rows):
+        lane = lax.broadcasted_iota(jnp.int32, (1, span * both), 1)
+        wanted = lane
+        for step, first, _ in segments(block):
+            base = across(me, step, groups) * capacity - first
+            wanted = jnp.where(lane >= first, lane + base, wanted)
+        column = jnp.concatenate([slot_column[rows, :]] * -(-span * both // LANES), axis=1)
+        hit = column[:, : span * both] == wanted
         return jnp.where(hit, 1.0, 0.0).astype(jnp.bfloat16)
 
-    def wait_home(pair):
-        far, near = steps_of(pair, groups)
-        homeward(2 * pair, far, FAR).wait_recv()
-
-        @pl.when(pair < own)
-        def _():
-            homeward(2 * pair + 1, near).wait_recv()
+    def wait_home(block):
+        each_pair(block, homeward, lambda copy: copy.wait_recv())
 
     everything = pl.ds(0, tokens)
 
@@ -490,29 +487,29 @@
                 place, source[rows, columns], preferred_element_type=jnp.float32
             )
 
-    @pl.loop(0, own)
-    def _(pair):
-        wait_home(pair)
-        gather(placement(pair, everything), returned, rows_of(pair))
+    @pl.loop(0, last)
+    def _(block):
+        wait_home(block)
+        gather(placement(block, everything), returned, rows_of(block))
 
     if spill:
         spill_back_copy.wait_recv()
         lane = lax.broadcasted_iota(jnp.int32, (tokens, lanes), 1)
         hit = tiled_lanes(spill_column[...], lanes) == lane
         gather(jnp.where(hit, 1.0, 0.0).astype(jnp.bfloat16), spill_home, pl.ds(0, lanes))
-    wait_home(own)
+    wait_home(last)
     chunk = min(LANES, tokens)
 
     @pl.loop(0, tokens // chunk)
     def _(part_of):
         rows = pl.ds(pl.multiple_of(part_of * chunk, chunk), chunk)
-        place = placement(own, rows)
+        place = placement(last, rows)
 
         @pl.loop(0, units // tile)
         def _(block):
             columns = pl.ds(pl.multiple_of(block * tile, tile), tile)
             back = total[rows, columns] + jnp.dot(
-                place, returned[rows_of(own), columns], preferred_element_type=jnp.float32
+                place, returned[rows_of(last), columns], preferred_element_type=jnp.float32
             )
             out_ref[rows, columns] = back.astype(jnp.bfloat16)
             terms = hidden[rows, columns].astype(jnp.float32) * back
@@ -536,22 +533,16 @@
     for hop in range(1, parts):
         gate_copy(hop, part).start()
 
-    @pl.loop(0, pairs)
-    def _(pair):
-        far, near = steps_of(pair, groups)
-        outward(2 * pair, far, FAR).wait_send()
-        homeward(2 * pair, far, FAR).wait_send()
+    @pl.loop(0, blocks)
+    def _(block):
+        each_pair(block, outward, lambda copy: copy.wait_send())
+        each_pair(block, homeward, lambda copy: copy.wait_send())
         for hop in range(1, parts):
-            sideways(pair, hop).wait_send()
-
-        @pl.when(pair < own)
-        def _():
-            outward(2 * pair + 1, near).wait_send()
-            homeward(2 * pair + 1, near).wait_send()
+            sideways(block, hop).wait_send()
 
     if spill:
         for hop in range(1, parts):
-            sideways(pairs, hop, relay_rows).wait_send()
+            sideways(blocks, hop, relay_rows).wait_send()
         place_copy.wait_send()
         spill_copy.wait_send()
         spill_back_copy.wait_send()

time: 162 us -> 165 us (1.019); the launches traced: 160 us -> 165 us
  Pallas kernels: 156 us -> 161 us
    pallas_call x1, Pallas kernels: 156 us -> 161 us  [call(): pl.pallas_call(functools.partial(kernel, groups, parts, capacity, tile, s...]
where the time goes in v4:
time: 165 us
  Pallas kernels  161 us (98%)
  other arithmetic  1.72 us (1%)
    pallas_call x1, Pallas kernels, call(): pl.pallas_call(functools.partial(kernel, groups, parts, capacity, tile, s...  161 us

profile of v4, /device:TPU:9, one launch (start us, length us, event | category | flops | bytes accessed | tf_op | source)
XLA Modules:
  0.0 165.0 jit_solution(471248207296567273)
XLA Ops:
  0.6 0.0 copy-start
  0.6 0.0 copy-start.1
  0.6 0.0 copy-start.2
  0.7 160.7 %shard_map.68 = (bf16[512,2048]{1,0:T(8,128)(2,1)S(1)}, f32[1,512]{1,0:T(1,128)S(1)}, s32[1,128]{1,0:T(1,128)}) custom-call(bf16[512,1536]{1,0:T(8,128)(2,1)} %grad_ref.1, bf16[512,2048]{1,0:T(8,128)(2,1)} %hidden_ref.1, s32[1,512]{1,0:T(1,128)} %bitcast.7, bf16[2048,3072]{1,0:T(8,128)(2,1)} %bitcast.5), custom_call_target="tpu_custom_call" | custom-call | tf_op jit(solution)/shard_map/pallas_call | solution.py:603
  162.0 0.0 copy-done
  162.0 0.0 copy-done.1
  162.0 0.0 copy-done.2
  162.1 0.0 copy-start.3
  162.1 0.7 copy-done.3
  162.7 1.7 %fusion = bf16[512,2048]{1,0:T(8,128)(2,1)} fusion(bf16[512,2048]{1,0:T(8,128)(2,1)S(1)} %get-tuple-element.46, f32[512]{0:T(512)S(1)} %copy-done.3), kind=kLoop, calls=%fused_computation.1 | loop fusion | flops 3145728 | bytes 4196352 | tf_op jit(solution)/shard_map/convert_element_type | solution.py:667
  164.5 0.6 copy.12
  (1 shorter events, 0.0 us)
Async XLA Ops:
  0.6 161.4 %copy-start = (bf16[512,2048]{1,0:T(8,128)(2,1)S(1)}, bf16[512,2048]{1,0:T(8,128)(2,1)}, u32[]{:S(2)}) copy-start(bf16[512,2048]{1,0:T(8,128)(2,1)} %hidden_ref.1) | copy-start | bytes 6291460
  0.6 161.4 %copy-start.1 = (bf16[512,1536]{1,0:T(8,128)(2,1)S(1)}, bf16[512,1536]{1,0:T(8,128)(2,1)}, u32[]{:S(2)}) copy-start(bf16[512,1536]{1,0:T(8,128)(2,1)} %grad_ref.1) | copy-start | bytes 4718596
  0.6 161.4 %copy-start.2 = (s32[512,1]{0,1:T(1,128)S(1)}, s32[512,1]{0,1:T(1,128)}, u32[]{:S(2)}) copy-start(s32[512,1]{0,1:T(1,128)} %param.10) | copy-start | bytes 6148
  162.1 0.7 copy-start.3

commit v5 on v3

--- a/solution.py
+++ b/solution.py
@@ -283,7 +283,7 @@
         spill_back_copy = to_mirror(
             spill_back, spill_home.at[pl.ds(0, spill)], spill_back_sem
         )
-        early = 3 * pairs // 8
+        early = 5 * pairs // 8
         pack(0, outgoing)
         pl.semaphore_wait(barrier, groups - 1 + parts - 1)
         send_pair(0)

time: 162 us -> 167 us (1.031); the launches traced: 160 us -> 167 us
  Pallas kernels: 156 us -> 163 us
    pallas_call x1, Pallas kernels: 156 us -> 163 us  [call(): pl.pallas_call(functools.partial(kernel, groups, parts, capacity, tile, s...]
where the time goes in v5:
time: 167 us
  Pallas kernels  163 us (98%)
  other arithmetic  1.72 us (1%)
    pallas_call x1, Pallas kernels, call(): pl.pallas_call(functools.partial(kernel, groups, parts, capacity, tile, s...  163 us

profile of v5, /device:TPU:9, one launch (start us, length us, event | category | flops | bytes accessed | tf_op | source)
XLA Modules:
  0.0 167.2 jit_solution(16209051267799255733)
XLA Ops:
  0.6 0.0 copy-start
  0.6 0.0 copy-start.1
  0.6 0.0 copy-start.2
  0.7 162.8 %shard_map.68 = (bf16[512,2048]{1,0:T(8,128)(2,1)S(1)}, f32[1,512]{1,0:T(1,128)S(1)}, s32[1,128]{1,0:T(1,128)}) custom-call(bf16[512,1536]{1,0:T(8,128)(2,1)} %grad_ref.1, bf16[512,2048]{1,0:T(8,128)(2,1)} %hidden_ref.1, s32[1,512]{1,0:T(1,128)} %bitcast.7, bf16[2048,3072]{1,0:T(8,128)(2,1)} %bitcast.5), custom_call_target="tpu_custom_call" | custom-call | tf_op jit(solution)/shard_map/pallas_call | solution.py:612
  164.2 0.0 copy-done
  164.2 0.0 copy-done.1
  164.2 0.0 copy-done.2
  164.2 0.0 copy-start.3
  164.2 0.7 copy-done.3
  164.9 1.7 %fusion = bf16[512,2048]{1,0:T(8,128)(2,1)} fusion(bf16[512,2048]{1,0:T(8,128)(2,1)S(1)} %get-tuple-element.46, f32[512]{0:T(512)S(1)} %copy-done.3), kind=kLoop, calls=%fused_computation.1 | loop fusion | flops 3145728 | bytes 4196352 | tf_op jit(solution)/shard_map/convert_element_type | solution.py:676
  166.6 0.6 copy.12
  (1 shorter events, 0.0 us)
Async XLA Ops:
  0.6 163.5 %copy-start = (bf16[512,2048]{1,0:T(8,128)(2,1)S(1)}, bf16[512,2048]{1,0:T(8,128)(2,1)}, u32[]{:S(2)}) copy-start(bf16[512,2048]{1,0:T(8,128)(2,1)} %hidden_ref.1) | copy-start | bytes 6291460
  0.6 163.5 %copy-start.1 = (bf16[512,1536]{1,0:T(8,128)(2,1)S(1)}, bf16[512,1536]{1,0:T(8,128)(2,1)}, u32[]{:S(2)}) copy-start(bf16[512,1536]{1,0:T(8,128)(2,1)} %grad_ref.1) | copy-start | bytes 4718596
  0.6 163.5 %copy-start.2 = (s32[512,1]{0,1:T(1,128)S(1)}, s32[512,1]{0,1:T(1,128)}, u32[]{:S(2)}) copy-start(s32[512,1]{0,1:T(1,128)} %param.10) | copy-start | bytes 6148
  164.2 0.7 copy-start.3
